TPU v7x, 512 devices: a whole 4x8x8 slice. The times are simulated.
512 devices in a mesh: graph: 16 (over z, core), config: 32 (over y, x).
Axes of the slice: x: 4, y: 8, z: 8, core: 2. Of those that a mesh axis runs over, the one named last changes fastest.
Arguments:
- features: bfloat16 [64, 8192, 128], P('config', 'graph'), may hold values from -6 to 6
- cotangent: bfloat16 [64, 8192, 128], P(None, ('graph', 'config')), may hold values from -6 to 6
- sage_weight: bfloat16 [2, 128, 128], replicated, may hold values from -0.5 to 0.5
- attn_weight: bfloat16 [4, 128, 128], replicated, may hold values from -0.5 to 0.5
- tile_vals: bfloat16 [192, 128, 128], P('graph'), may hold values from -0.375 to 0.375
- tile_dst: int32 [192], P('graph'), may hold values from 0 to 3
- tile_src: int32 [192], P('graph'), may hold values from 0 to 3
- tile_count: int32 [16], P('graph'), may hold values from 3 to 12, as said below
- hub_ids: int32 [128], P('graph'), may hold values from 0 to 8191, as said below
- hub_weight: bfloat16 [8192, 128], P('graph'), may hold values from -0.5 to 0.5
Outputs:
- layer_out: bfloat16 [64, 8192, 128], P(None, ('graph', 'config'))
- grad_features: bfloat16 [64, 8192, 128], P('config', 'graph')
- grad_weights: float32 [16, 6, 128, 128], P('graph')
Inputs may be any that keep to these rules, and one draw needn't show every extreme that they name: Slot t of slab g (t counted within the slab) is live when t < tile_count[g]; some slab has all 12 slots live. `hub_ids`: entries g * 8 to (g+1) * 8 - 1 are distinct nodes of slab g.
All inputs are finite; a program needn't handle non-finite values.
Results may differ from a plain program's by a relative error of at most 0.024.
Values may be sent and summed in bfloat16 or wider, within the bound.
A program may use at most 64 MiB of HBM per device.

v0:
```python
import math
import jax
import jax.numpy as jnp
from jax import lax
from jax.sharding import PartitionSpec as P

HEADS = 4
CAP = 20.0


def attend(queries, key_rows, value_rows):
    layout_count, node_count, feature_width = queries.shape
    head_size = feature_width // HEADS
    split = (layout_count, node_count, HEADS, head_size)
    query_b = queries.reshape(split)
    key_b = key_rows.reshape(split)
    value_b = value_rows.reshape(split)
    scores = jnp.einsum(
        "lkhd,mkhd->khlm", query_b, key_b, preferred_element_type=jnp.float32
    ) / math.sqrt(head_size)
    capped = CAP * jnp.tanh(scores / CAP)
    weights = jnp.exp(capped)
    attention = weights / jnp.sum(weights, axis=-1, keepdims=True)
    attention = attention.astype(value_b.dtype)
    mixture = jnp.einsum("khlm,mkhd->lkhd", attention, value_b, preferred_element_type=jnp.float32)
    return mixture.reshape(layout_count, node_count, feature_width).astype(queries.dtype)


def project(flat_rows, weight):
    return jnp.dot(flat_rows, weight, preferred_element_type=jnp.float32)


def project_back(flat_rows, weight):
    return jnp.dot(flat_rows, weight.T, preferred_element_type=jnp.float32)


def outer_sum(left_rows, right_rows):
    return jnp.dot(left_rows.T, right_rows, preferred_element_type=jnp.float32)


def sage_forward(feats, aggregate, sage_weight):
    shaped = feats.shape
    width_f = shaped[-1]
    pre_acts = project(feats.reshape(-1, width_f), sage_weight[0]) + project(
        aggregate.reshape(-1, width_f), sage_weight[1]
    )
    hidden = jax.nn.silu(pre_acts).astype(jnp.bfloat16)
    return (pre_acts.reshape(shaped), hidden.reshape(shaped))


def node_forward(hidden, attn_weight):
    shaped = hidden.shape
    width_f = shaped[-1]
    three = (shaped[0], -1, width_f)
    flat_hidden = hidden.reshape(-1, width_f)
    queries = project(flat_hidden, attn_weight[0]).astype(jnp.bfloat16)
    key_rows = project(flat_hidden, attn_weight[1]).astype(jnp.bfloat16)
    value_rows = project(flat_hidden, attn_weight[2]).astype(jnp.bfloat16)
    mixture = attend(queries.reshape(three), key_rows.reshape(three), value_rows.reshape(three))
    output = (
        flat_hidden.astype(jnp.float32) + project(mixture.reshape(-1, width_f), attn_weight[3])
    ).astype(jnp.bfloat16)
    return (
        output.reshape(shaped),
        queries.reshape(shaped),
        key_rows.reshape(shaped),
        value_rows.reshape(shaped),
        mixture.reshape(shaped),
    )


def node_backward(cot_rows, hidden, queries, key_rows, value_rows, mixture, attn_weight):
    shaped = hidden.shape
    width_f = shaped[-1]
    three = (shaped[0], -1, width_f)
    flat_cot = cot_rows.reshape(-1, width_f)
    grad_mix = project_back(flat_cot, attn_weight[3]).astype(jnp.bfloat16)
    grad_wo = outer_sum(mixture.reshape(-1, width_f), flat_cot)
    unused, pullback = jax.vjp(attend, queries, key_rows, value_rows)
    grad_q, grad_k, grad_v = pullback(grad_mix.reshape(three))
    flat_q = grad_q.reshape(-1, width_f)
    flat_k = grad_k.reshape(-1, width_f)
    flat_v = grad_v.reshape(-1, width_f)
    grad_hidden = (
        flat_cot.astype(jnp.float32)
        + project_back(flat_q, attn_weight[0])
        + project_back(flat_k, attn_weight[1])
        + project_back(flat_v, attn_weight[2])
    ).astype(jnp.bfloat16)
    flat_hidden = hidden.reshape(-1, width_f)
    grads = jnp.stack(
        [
            outer_sum(flat_hidden, flat_q),
            outer_sum(flat_hidden, flat_k),
            outer_sum(flat_hidden, flat_v),
            grad_wo,
        ]
    )
    return (grad_hidden.reshape(shaped), grads)


def sage_backward(grad_hidden, pre_acts, feats, aggregate, sage_weight):
    shaped = feats.shape
    width_f = shaped[-1]
    flat_pre = pre_acts.reshape(-1, width_f)
    sigmoid_pre = jax.nn.sigmoid(flat_pre)
    grad_pre = (
        grad_hidden.reshape(-1, width_f).astype(jnp.float32)
        * sigmoid_pre
        * (1.0 + flat_pre * (1.0 - sigmoid_pre))
    ).astype(jnp.bfloat16)
    grads = jnp.stack(
        [
            outer_sum(feats.reshape(-1, width_f), grad_pre),
            outer_sum(aggregate.reshape(-1, width_f), grad_pre),
        ]
    )
    grad_self = project_back(grad_pre, sage_weight[0]).astype(jnp.bfloat16).reshape(shaped)
    grad_agg = project_back(grad_pre, sage_weight[1]).astype(jnp.bfloat16).reshape(shaped)
    return (grad_self, grad_agg, grads)


def tile_forward(source, tile_vals, tile_src, tile_dst, live):
    layout_count, node_count, width_f = source.shape
    tile_size = tile_vals.shape[1]
    block_count = node_count // tile_size
    blocks = source.reshape(layout_count, block_count, tile_size, width_f)[:, tile_src]
    products = jnp.einsum("tij,ltjf->tlif", tile_vals, blocks, preferred_element_type=jnp.float32)
    products = products * live[:, None, None, None]
    summed = jax.ops.segment_sum(products, tile_dst, num_segments=block_count)
    return summed.transpose(1, 0, 2, 3).reshape(layout_count, node_count, width_f)


def tile_backward(grad_agg, tile_vals, tile_dst, tile_src, live):
    layout_count, node_count, width_f = grad_agg.shape
    tile_size = tile_vals.shape[1]
    block_count = node_count // tile_size
    blocks = grad_agg.reshape(layout_count, block_count, tile_size, width_f)[:, tile_dst]
    products = jnp.einsum("tij,ltif->tljf", tile_vals, blocks, preferred_element_type=jnp.float32)
    products = products * live[:, None, None, None]
    summed = jax.ops.segment_sum(products, tile_src, num_segments=block_count)
    return summed.transpose(1, 0, 2, 3).reshape(layout_count, node_count, width_f)


def flatten_nodes(arrays):
    return tuple((item.reshape(item.shape[0], -1, item.shape[-1]) for item in arrays))


def local(
    features,
    cotangent,
    sage_weight,
    attn_weight,
    tile_vals,
    tile_dst,
    tile_src,
    tile_count,
    hub_ids,
    hub_weight,
):
    layout_dev, node_dev, width_f = features.shape
    config_count = lax.axis_size("config")
    node_share = node_dev // config_count
    slab_index = lax.axis_index("graph")
    hub_local = hub_ids - slab_index * node_dev
    live = (jnp.arange(tile_dst.shape[0], dtype=jnp.int32) < tile_count[0]).astype(jnp.float32)
    local_hubs = features[:, hub_local]
    columns = hub_weight
    hub_sum = jnp.einsum(
        "nj,ljf->lnf",
        columns,
        lax.all_gather(local_hubs, "graph", axis=1, tiled=True),
        preferred_element_type=jnp.float32,
    )
    aggregate = (tile_forward(features, tile_vals, tile_src, tile_dst, live) + hub_sum).astype(
        jnp.bfloat16
    )
    split_shape = (layout_dev, config_count, node_share, width_f)
    back_shape = (layout_dev * config_count, 1, node_share, width_f)
    received = (
        lax.all_to_all(
            features.reshape(split_shape), "config", split_axis=1, concat_axis=0, tiled=True
        ),
        lax.all_to_all(
            aggregate.reshape(split_shape), "config", split_axis=1, concat_axis=0, tiled=True
        ),
    )
    pre_in, hidden_in = sage_forward(received[0], received[1], sage_weight)
    results = (received[0], received[1], pre_in, hidden_in) + node_forward(hidden_in, attn_weight)
    feats_node, agg_node, pre_node, hidden_node, output, queries, key_rows, value_rows, mixture = (
        flatten_nodes(results)
    )
    grad_hidden, attn_grads = node_backward(
        cotangent, hidden_node, queries, key_rows, value_rows, mixture, attn_weight
    )
    self_node, aggr_node, sage_grads = sage_backward(
        grad_hidden, pre_node, feats_node, agg_node, sage_weight
    )
    self_back, agg_back = (
        lax.all_to_all(
            self_node.reshape(back_shape), "config", split_axis=0, concat_axis=1, tiled=True
        ),
        lax.all_to_all(
            aggr_node.reshape(back_shape), "config", split_axis=0, concat_axis=1, tiled=True
        ),
    )
    grad_self = self_back.reshape(layout_dev, node_dev, width_f)
    grad_agg = agg_back.reshape(layout_dev, node_dev, width_f)
    back_rows = tile_backward(grad_agg, tile_vals, tile_dst, tile_src, live)
    columns = hub_weight
    hub_grads = lax.psum_scatter(
        jnp.einsum("nj,lnf->jlf", columns, grad_agg, preferred_element_type=jnp.float32).astype(
            jnp.bfloat16
        ),
        "graph",
        scatter_dimension=0,
        tiled=True,
    ).astype(jnp.float32)
    totals = grad_self.astype(jnp.float32) + back_rows
    totals = totals.at[:, hub_local].add(jnp.transpose(hub_grads, (1, 0, 2)))
    grad_features = totals.astype(jnp.bfloat16)
    partial_grads = jnp.concatenate([sage_grads, attn_grads], axis=0)
    summed = lax.psum(partial_grads.astype(jnp.bfloat16), "config").astype(jnp.float32)
    scale = 1.0 / math.sqrt(layout_dev * config_count * node_dev)
    return (output, grad_features, (summed * scale)[None])


def solution(mesh):
    return jax.shard_map(
        local,
        mesh=mesh,
        in_specs=(
            P("config", "graph", None),
            P(None, ("graph", "config"), None),
            P(),
            P(),
            P("graph", None, None),
            P("graph"),
            P("graph"),
            P("graph"),
            P("graph"),
            P("graph", None),
        ),
        out_specs=(
            P(None, ("graph", "config"), None),
            P("config", "graph", None),
            P("graph", None, None, None),
        ),
        check_vma=False,
    )
```

profile of v0, /device:TPU:1, one launch (start us, length us, event | category | flops | bytes accessed | tf_op | source)
XLA Modules:
  0.0 400.2 jit_solution(9092489679401032103)
XLA Ops:
  8.0 1.7 copy.116
  9.7 10.5 %all-to-all-start = ((bf16[2,32,16,128]{3,2,0,1:T(8,128)(2,1)}), bf16[2,32,16,128]{3,2,0,1:T(8,128)(2,1)S(1)}, u32[]{:S(2)}, u32[]{:S(2)}) async-start(bf16[2,32,16,128]{3,2,0,1:T(8,128)(2,1)} %copy.116), calls=%async_computation | async-start | bytes 524288 | tf_op jit(solution)/shard_map/all_to_all | solution.py:181
  24.4 1.6 gather_fusion
  27.7 1.9 copy.118
  29.6 1.8 scatter_fusion
  32.0 24.1 %all-gather = bf16[2,128,128]{2,1,0:T(8,128)(2,1)S(1)} all-gather(bf16[2,8,128]{2,1,0:T(8,128)(2,1)S(1)} %bitcast.206), channel_id=2, replica_groups=mesh['graph'=16,'config'=32] {'graph'}, dimensions={1}, use_global_device_ids=true | all-gather | bytes 69632 | tf_op jit(solution)/shard_map/all_gather | solution.py:172
  57.2 9.8 %all-to-all-start.1 = ((bf16[2,32,16,128]{3,2,0,1:T(8,128)(2,1)}), bf16[2,32,16,128]{3,2,0,1:T(8,128)(2,1)S(1)}, u32[]{:S(2)}, u32[]{:S(2)}) async-start(bf16[2,32,16,128]{3,2,0,1:T(8,128)(2,1)} %copy.121), calls=%async_computation.1 | async-start | bytes 524288 | tf_op jit(solution)/shard_map/all_to_all | solution.py:184
  71.1 7.6 %all-to-all-done.1 = bf16[2,32,16,128]{3,2,0,1:T(8,128)(2,1)S(1)} async-done(((bf16[2,32,16,128]{3,2,0,1:T(8,128)(2,1)}), bf16[2,32,16,128]{3,2,0,1:T(8,128)(2,1)S(1)}, u32[]{:S(2)}, u32[]{:S(2)}) %all-to-all-start.1) | async-done | bytes 262176 | tf_op jit(solution)/shard_map/all_to_all | solution.py:184
  82.7 2.1 reshape_reshape.25
  84.8 1.8 copy.123
  86.6 3.2 fusion.7
  91.5 1.9 copy.124
  93.4 2.8 fusion.6
  101.8 1.6 copy.134
  104.0 2.5 copy.131
  108.1 2.5 copy.137
  117.0 4.4 %all-to-all-start.3 = ((bf16[64,1,16,128]{3,2,1,0:T(8,128)(2,1)}), bf16[64,1,16,128]{3,2,1,0:T(8,128)(2,1)S(1)}, u32[]{:S(2)}, u32[]{:S(2)}) async-start(bf16[64,1,16,128]{3,2,1,0:T(8,128)(2,1)} %bitcast.37), calls=%async_computation.3 | async-start | bytes 524288 | tf_op jit(solution)/shard_map/all_to_all | solution.py:203
  124.7 1.7 fusion.13
  127.3 4.5 %all-to-all-done.3 = bf16[64,1,16,128]{3,2,1,0:T(8,128)(2,1)S(1)} async-done(((bf16[64,1,16,128]{3,2,1,0:T(8,128)(2,1)}), bf16[64,1,16,128]{3,2,1,0:T(8,128)(2,1)S(1)}, u32[]{:S(2)}, u32[]{:S(2)}) %all-to-all-start.3) | async-done | bytes 262176 | tf_op jit(solution)/shard_map/all_to_all | solution.py:203
  131.8 5.2 %all-to-all-start.2 = ((bf16[64,1,16,128]{3,2,1,0:T(8,128)(2,1)}), bf16[64,1,16,128]{3,2,1,0:T(8,128)(2,1)S(1)}, u32[]{:S(2)}, u32[]{:S(2)}) async-start(bf16[64,1,16,128]{3,2,1,0:T(8,128)(2,1)} %bitcast.32), calls=%async_computation.2 | async-start | bytes 524288 | tf_op jit(solution)/shard_map/all_to_all | solution.py:200
  137.1 136.0 %all-reduce.4.cloned.1.call-done = bf16[6,128,128]{1,2,0:T(8,128)(2,1)} async-done(((bf16[6,128,128]{1,2,0:T(8,128)(2,1)}), bf16[6,128,128]{1,2,0:T(8,128)(2,1)}) %all-reduce.4.cloned.1.call-update) | async-done | bytes 196624 | tf_op jit(solution)/shard_map/psum | solution.py:223
  277.3 1.9 copy.143
  279.3 1.8 scatter_fusion.1
  283.9 106.4 %all-reduce.6.cloned.1.call-done = bf16[128,2,128]{2,1,0:T(2,128)(2,1)} async-done(((bf16[128,2,128]{2,1,0:T(2,128)(2,1)}), bf16[128,2,128]{2,1,0:T(2,128)(2,1)}) %all-reduce.6.cloned.1.call-update) | async-done | bytes 65552
  (108 shorter events, 43.3 us)
Async XLA Ops:
  8.0 18.1 %copy-start = (bf16[12,128,128]{2,1,0:T(8,128)(2,1)S(1)}, bf16[12,128,128]{2,1,0:T(8,128)(2,1)}, u32[]{:S(2)}) copy-start(bf16[12,128,128]{2,1,0:T(8,128)(2,1)} %param.14) | copy-start | bytes 1179652
  9.7 47.5 %all-to-all-start = ((bf16[2,32,16,128]{3,2,0,1:T(8,128)(2,1)}), bf16[2,32,16,128]{3,2,0,1:T(8,128)(2,1)S(1)}, u32[]{:S(2)}, u32[]{:S(2)}) async-start(bf16[2,32,16,128]{3,2,0,1:T(8,128)(2,1)} %copy.116), calls=%async_computation | async-start | bytes 524288 | tf_op jit(solution)/shard_map/all_to_all | solution.py:181
  27.7 1.9 copy-start.17
  31.5 24.6 %copy-start.9 = (bf16[512,128]{1,0:T(8,128)(2,1)S(1)}, bf16[512,128]{1,0:T(8,128)(2,1)}, u32[]{:S(2)}) copy-start(bf16[512,128]{1,0:T(8,128)(2,1)} %param.19) | copy-start | bytes 393220
  31.7 35.3 %copy-start.1 = (bf16[64,16,128]{2,1,0:T(8,128)(2,1)S(1)}, bf16[64,16,128]{2,1,0:T(8,128)(2,1)}, u32[]{:S(2)}) copy-start(bf16[64,16,128]{2,1,0:T(8,128)(2,1)} %param.11) | copy-start | bytes 786436
  31.7 35.3 %copy-start.10 = (bf16[4,128,128]{2,1,0:T(8,128)(2,1)S(1)}, bf16[4,128,128]{2,1,0:T(8,128)(2,1)}, u32[]{:S(2)}) copy-start(bf16[4,128,128]{2,1,0:T(8,128)(2,1)} %param.13) | copy-start | bytes 393220
  57.2 13.6 %copy-start.13 = (bf16[2,128,128]{2,1,0:T(8,128)(2,1)S(1)}, bf16[2,128,128]{2,1,0:T(8,128)(2,1)}, u32[]{:S(2)}) copy-start(bf16[2,128,128]{2,1,0:T(8,128)(2,1)} %param.12) | copy-start | bytes 196612
  57.2 21.5 %all-to-all-start.1 = ((bf16[2,32,16,128]{3,2,0,1:T(8,128)(2,1)}), bf16[2,32,16,128]{3,2,0,1:T(8,128)(2,1)S(1)}, u32[]{:S(2)}, u32[]{:S(2)}) async-start(bf16[2,32,16,128]{3,2,0,1:T(8,128)(2,1)} %copy.121), calls=%async_computation.1 | async-start | bytes 524288 | tf_op jit(solution)/shard_map/all_to_all | solution.py:184
  78.7 2.2 copy-start.7
  93.4 2.9 copy-start.2
  93.4 2.9 copy-start.16
  97.2 1.5 copy-start.3
  98.7 2.7 copy-start.4
  99.9 1.9 copy-start.5
  103.4 3.6 copy-start.11
  113.1 1.8 copy-start.14
  113.1 2.8 copy-start.8
  114.6 2.1 copy-start.6
  117.0 14.8 %all-to-all-start.3 = ((bf16[64,1,16,128]{3,2,1,0:T(8,128)(2,1)}), bf16[64,1,16,128]{3,2,1,0:T(8,128)(2,1)S(1)}, u32[]{:S(2)}, u32[]{:S(2)}) async-start(bf16[64,1,16,128]{3,2,1,0:T(8,128)(2,1)} %bitcast.37), calls=%async_computation.3 | async-start | bytes 524288 | tf_op jit(solution)/shard_map/all_to_all | solution.py:203
  121.4 151.7 %all-reduce.4.cloned.1.call-start = ((), (), s32[]{:S(2)}) async-start(), calls=%async_computation.4 | async-start | bytes 393216 | tf_op jit(solution)/shard_map/psum | solution.py:223
  121.8 0.7 copy-start.12
  131.8 149.3 %all-to-all-start.2 = ((bf16[64,1,16,128]{3,2,1,0:T(8,128)(2,1)}), bf16[64,1,16,128]{3,2,1,0:T(8,128)(2,1)S(1)}, u32[]{:S(2)}, u32[]{:S(2)}) async-start(bf16[64,1,16,128]{3,2,1,0:T(8,128)(2,1)} %bitcast.32), calls=%async_computation.2 | async-start | bytes 524288 | tf_op jit(solution)/shard_map/all_to_all | solution.py:200
  137.0 253.3 %all-reduce.6.cloned.1.call-start = ((), (), s32[]{:S(2)}) async-start(), calls=%async_computation.5 | async-start | bytes 131072
  277.3 1.9 copy-start.18
  (1 other events, 0.6 us)
Sparse Core Ops, SparseCore 0:
  126.0 147.0 all-reduce.3
Sparse Core Ops, SparseCore 1:
  283.4 106.9 all-reduce.5
where the time goes:
time: 401 us; the launch traced here: 400 us
  waiting for transfers between devices  255 us (64%)
  local copies, waits for them, and re-layouts  36.5 us (9%)
  starting transfers between devices  30 us (7%)
  matrix products  27.2 us (7%)
  blocking collectives  24.1 us (6%)
  between operations  17.4 us (4%)
  other arithmetic  10.5 us (3%)
    psum x1, waiting for transfers between devices, local(): lax.psum(partial_grads.astype(jnp.bfloat16), 'config').astype(jnp.float32)  136 us
    unnamed x3, waiting for transfers between devices  106 us
    all_gather x1, blocking collectives, local(): lax.all_gather(local_hubs, 'graph', axis=1, tiled=True)  24.1 us
    all_to_all x1, starting transfers between devices, local(): lax.all_to_all(features.reshape(split_shape), 'config', split_axis=1, con...  10.5 us
    all_to_all x1, starting transfers between devices, local(): lax.all_to_all(aggregate.reshape(split_shape), 'config', split_axis=1, co...  9.81 us
  transfers between devices with their start and end apart: 6, of which 4 were waited for; matrix products, arithmetic and copies ran while one was open for 7% of the time, Pallas kernels for 0%

commit v1 on v0

--- a/solution.py
+++ b/solution.py
@@ -220,7 +220,9 @@
     totals = totals.at[:, hub_local].add(jnp.transpose(hub_grads, (1, 0, 2)))
     grad_features = totals.astype(jnp.bfloat16)
     partial_grads = jnp.concatenate([sage_grads, attn_grads], axis=0)
-    summed = lax.psum(partial_grads.astype(jnp.bfloat16), "config").astype(jnp.float32)
+    summed = jnp.sum(lax.all_gather(partial_grads.astype(jnp.bfloat16), "config"), axis=0).astype(
+        jnp.float32
+    )
     scale = 1.0 / math.sqrt(layout_dev * config_count * node_dev)
     return (output, grad_features, (summed * scale)[None])
 

time: 401 us -> 253 us (0.63)
  waiting for transfers between devices: 255 us -> 96.2 us
  matrix products: 27.2 us -> 32.2 us
    psum x1 -> x0, waiting for transfers between devices: 136 us -> none  [local(): lax.psum(partial_grads.astype(jnp.bfloat16), 'config').astype(jnp.float32)]
    unnamed x3, waiting for transfers between devices: 106 us -> 78.7 us
    reduce_sum x0 -> x1, other arithmetic: none -> 4.19 us  [local(): jnp.sum(lax.all_gather(partial_grads.astype(jnp.bfloat16), 'config'), axi...]
  transfers between devices with their start and end apart: 6 -> 6, of which waited for: 4 -> 4; matrix products, arithmetic and copies ran while one was open for 7% -> 14% of each run, Pallas kernels for 0% -> 0%
where the time goes in v1:
time: 253 us; the launch traced here: 252 us
  waiting for transfers between devices  96.2 us (38%)
  local copies, waits for them, and re-layouts  37.9 us (15%)
  matrix products  32.2 us (13%)
  starting transfers between devices  30 us (12%)
  blocking collectives  24.1 us (10%)
  between operations  17.4 us (7%)
  other arithmetic  13.7 us (5%)
    unnamed x3, waiting for transfers between devices  78.7 us
    all_gather x1, blocking collectives, local(): lax.all_gather(local_hubs, 'graph', axis=1, tiled=True)  24.1 us
    all_to_all x1, starting transfers between devices, local(): lax.all_to_all(features.reshape(split_shape), 'config', split_axis=1, con...  10.5 us
    all_to_all x1, starting transfers between devices, local(): lax.all_to_all(aggregate.reshape(split_shape), 'config', split_axis=1, co...  9.81 us
    all_to_all x1, waiting for transfers between devices, local(): lax.all_to_all(aggregate.reshape(split_shape), 'config', split_axis=1, co...  8.94 us
    all_to_all x1, waiting for transfers between devices, local(): lax.all_to_all(aggr_node.reshape(back_shape), 'config', split_axis=0, con...  8 us
    dot_general x3, matrix products, attend(): jnp.einsum('khlm,mkhd->lkhd', attention, value_b, preferred_element_type=...  7.03 us
    dot_general x6, matrix products, project_back(): return jnp.dot(flat_rows, weight.T, preferred_element_type=jnp.float32)  6.9 us
  transfers between devices with their start and end apart: 6, of which 4 were waited for; matrix products, arithmetic and copies ran while one was open for 14% of the time, Pallas kernels for 0%

profile of v1, /device:TPU:1, one launch (start us, length us, event | category | flops | bytes accessed | tf_op | source)
XLA Modules:
  0.0 251.5 jit_solution(9683892311877536994)
XLA Ops:
  8.0 1.7 copy.113
  9.7 10.5 %all-to-all-start = ((bf16[2,32,16,128]{3,2,0,1:T(8,128)(2,1)}), bf16[2,32,16,128]{3,2,0,1:T(8,128)(2,1)S(1)}, u32[]{:S(2)}, u32[]{:S(2)}) async-start(bf16[2,32,16,128]{3,2,0,1:T(8,128)(2,1)} %copy.113), calls=%async_computation | async-start | bytes 524288 | tf_op jit(solution)/shard_map/all_to_all | solution.py:181
  27.7 1.9 copy.115
  29.6 1.8 scatter_fusion
  32.0 24.1 %all-gather = bf16[2,128,128]{2,1,0:T(8,128)(2,1)S(1)} all-gather(bf16[2,8,128]{2,1,0:T(8,128)(2,1)S(1)} %bitcast.206), channel_id=2, replica_groups=mesh['graph'=16,'config'=32] {'graph'}, dimensions={1}, use_global_device_ids=true | all-gather | bytes 69632 | tf_op jit(solution)/shard_map/all_gather | solution.py:172
  57.2 9.8 %all-to-all-start.1 = ((bf16[2,32,16,128]{3,2,0,1:T(8,128)(2,1)}), bf16[2,32,16,128]{3,2,0,1:T(8,128)(2,1)S(1)}, u32[]{:S(2)}, u32[]{:S(2)}) async-start(bf16[2,32,16,128]{3,2,0,1:T(8,128)(2,1)} %copy.118), calls=%async_computation.1 | async-start | bytes 524288 | tf_op jit(solution)/shard_map/all_to_all | solution.py:184
  67.7 1.8 copy.124
  69.8 8.9 %all-to-all-done.1 = bf16[2,32,16,128]{3,2,0,1:T(8,128)(2,1)S(1)} async-done(((bf16[2,32,16,128]{3,2,0,1:T(8,128)(2,1)}), bf16[2,32,16,128]{3,2,0,1:T(8,128)(2,1)S(1)}, u32[]{:S(2)}, u32[]{:S(2)}) %all-to-all-start.1) | async-done | bytes 262176 | tf_op jit(solution)/shard_map/all_to_all | solution.py:184
  84.4 2.2 fusion.7
  88.3 1.8 copy.121
  90.1 3.1 %fusion.6 = (f32[16,4,64]{2,1,0:T(4,128)S(1)}, bf16[16,4,64,64]{2,3,1,0:T(8,128)(2,1)S(1)}, bf16[16,4,64,64]{2,3,1,0:T(8,128)(2,1)S(1)}) fusion(f32[16,4,64,64]{2,3,1,0:T(8,128)} %get-tuple-element.20, f32[16,4,64]{2,1,0:T(4,128)} %multiply_divide_fusion, f32[16,4,64]{2,1,0:T(4,128)} %copy-done.17, bf16[16,4,32,64]{3,2,1,0:T(8,128)(2,1)} %copy.124, ...), kind=kOutput, calls=%fused_computation.14 | convolution fusion | flops 18870272 | bytes 2670592 | tf_op jit(solution)/shard_map/transpose(jvp(khlm,mkhd->lkhd))/dot_general | solution.py:25
  96.9 2.5 %copy.131 = bf16[64,16,4,32]{3,2,1,0:T(4,128)(2,1)S(1)} copy(bf16[64,16,4,32]{0,3,2,1:T(8,128)(2,1)} %fusion.9) | data formatting | bytes 524288 | tf_op jit(solution)/shard_map/transpose(jvp(lkhd,mkhd->khlm))/convert_element_type | solution.py:18
  100.0 2.5 %copy.128 = bf16[64,16,4,32]{3,2,1,0:T(4,128)(2,1)S(1)} copy(bf16[64,16,4,32]{0,3,2,1:T(8,128)(2,1)} %fusion.8) | data formatting | bytes 524288 | tf_op jit(solution)/shard_map/transpose(jvp(lkhd,mkhd->khlm))/convert_element_type | solution.py:18
  103.7 2.0 convolution_add_fusion.2
  105.7 2.5 fusion.10
  108.2 2.7 %copy.134 = bf16[64,16,4,32]{3,2,1,0:T(4,128)(2,1)S(1)} copy(bf16[64,16,4,32]{0,3,2,1:T(8,128)(2,1)} %fusion.10) | data formatting | bytes 524288 | tf_op jit(solution)/shard_map/transpose(jvp(khlm,mkhd->lkhd))/convert_element_type | solution.py:25
  119.6 4.5 %all-to-all-start.3 = ((bf16[64,1,16,128]{3,2,1,0:T(8,128)(2,1)}), bf16[64,1,16,128]{3,2,1,0:T(8,128)(2,1)S(1)}, u32[]{:S(2)}, u32[]{:S(2)}) async-start(bf16[64,1,16,128]{3,2,1,0:T(8,128)(2,1)} %bitcast.37), calls=%async_computation.3 | async-start | bytes 524288 | tf_op jit(solution)/shard_map/all_to_all | solution.py:203
  126.5 8.0 %all-to-all-done.3 = bf16[64,1,16,128]{3,2,1,0:T(8,128)(2,1)S(1)} async-done(((bf16[64,1,16,128]{3,2,1,0:T(8,128)(2,1)}), bf16[64,1,16,128]{3,2,1,0:T(8,128)(2,1)S(1)}, u32[]{:S(2)}, u32[]{:S(2)}) %all-to-all-start.3) | async-done | bytes 262176 | tf_op jit(solution)/shard_map/all_to_all | solution.py:203
  136.6 1.7 copy.153
  141.2 5.2 %all-to-all-start.2 = ((bf16[64,1,16,128]{3,2,1,0:T(8,128)(2,1)}), bf16[64,1,16,128]{3,2,1,0:T(8,128)(2,1)S(1)}, u32[]{:S(2)}, u32[]{:S(2)}) async-start(bf16[64,1,16,128]{3,2,1,0:T(8,128)(2,1)} %bitcast.32), calls=%async_computation.2 | async-start | bytes 524288 | tf_op jit(solution)/shard_map/all_to_all | solution.py:200
  152.5 1.9 copy.140
  154.5 1.8 scatter_fusion.1
  157.7 78.7 %all-reduce.3.cloned.1.call-done = bf16[128,2,128]{2,1,0:T(2,128)(2,1)} async-done(((bf16[128,2,128]{2,1,0:T(2,128)(2,1)}), bf16[128,2,128]{2,1,0:T(2,128)(2,1)}) %all-reduce.3.cloned.1.call-update) | async-done | bytes 65552
  238.8 4.2 %reduce_sum.40 = bf16[6,128,128]{2,1,0:T(8,128)(2,1)S(1)} reduce(bf16[32,6,128,128]{3,2,1,0:T(8,128)(2,1)} %all-gather.3.cloned.1.call-done, bf16[]{:T(256)} %constant.35.clone.1), dimensions={0}, to_apply=%region_6.7 | reduce | flops 3047424 | bytes 6488066 | tf_op jit(solution)/shard_map/reduce_sum | solution.py:223
  (115 shorter events, 48.1 us)
Async XLA Ops:
  8.0 18.1 %copy-start = (bf16[12,128,128]{2,1,0:T(8,128)(2,1)S(1)}, bf16[12,128,128]{2,1,0:T(8,128)(2,1)}, u32[]{:S(2)}) copy-start(bf16[12,128,128]{2,1,0:T(8,128)(2,1)} %param.14) | copy-start | bytes 1179652
  9.7 47.5 %all-to-all-start = ((bf16[2,32,16,128]{3,2,0,1:T(8,128)(2,1)}), bf16[2,32,16,128]{3,2,0,1:T(8,128)(2,1)S(1)}, u32[]{:S(2)}, u32[]{:S(2)}) async-start(bf16[2,32,16,128]{3,2,0,1:T(8,128)(2,1)} %copy.113), calls=%async_computation | async-start | bytes 524288 | tf_op jit(solution)/shard_map/all_to_all | solution.py:181
  27.7 1.9 copy-start.19
  31.5 24.6 %copy-start.11 = (bf16[512,128]{1,0:T(8,128)(2,1)S(1)}, bf16[512,128]{1,0:T(8,128)(2,1)}, u32[]{:S(2)}) copy-start(bf16[512,128]{1,0:T(8,128)(2,1)} %param.19) | copy-start | bytes 393220
  31.7 35.3 %copy-start.1 = (bf16[64,16,128]{2,1,0:T(8,128)(2,1)S(1)}, bf16[64,16,128]{2,1,0:T(8,128)(2,1)}, u32[]{:S(2)}) copy-start(bf16[64,16,128]{2,1,0:T(8,128)(2,1)} %param.11) | copy-start | bytes 786436
  31.7 35.3 %copy-start.13 = (bf16[4,128,128]{2,1,0:T(8,128)(2,1)S(1)}, bf16[4,128,128]{2,1,0:T(8,128)(2,1)}, u32[]{:S(2)}) copy-start(bf16[4,128,128]{2,1,0:T(8,128)(2,1)} %param.13) | copy-start | bytes 393220
  57.2 12.3 %copy-start.14 = (bf16[2,128,128]{2,1,0:T(8,128)(2,1)S(1)}, bf16[2,128,128]{2,1,0:T(8,128)(2,1)}, u32[]{:S(2)}) copy-start(bf16[2,128,128]{2,1,0:T(8,128)(2,1)} %param.12) | copy-start | bytes 196612
  57.2 21.5 %all-to-all-start.1 = ((bf16[2,32,16,128]{3,2,0,1:T(8,128)(2,1)}), bf16[2,32,16,128]{3,2,0,1:T(8,128)(2,1)S(1)}, u32[]{:S(2)}, u32[]{:S(2)}) async-start(bf16[2,32,16,128]{3,2,0,1:T(8,128)(2,1)} %copy.118), calls=%async_computation.1 | async-start | bytes 524288 | tf_op jit(solution)/shard_map/all_to_all | solution.py:184
  78.7 2.4 copy-start.9
  82.8 3.8 %copy-start.4 = (bf16[64,16,4,32]{0,3,2,1:T(8,128)(2,1)}, bf16[64,16,4,32]{0,3,2,1:T(8,128)(2,1)S(1)}, u32[]{:S(2)}) copy-start(bf16[64,16,4,32]{0,3,2,1:T(8,128)(2,1)S(1)} %copy.119) | copy-start | bytes 786436
  84.4 3.9 %copy-start.6 = (bf16[64,16,4,32]{0,3,2,1:T(8,128)(2,1)}, bf16[64,16,4,32]{0,3,2,1:T(8,128)(2,1)S(1)}, u32[]{:S(2)}) copy-start(bf16[64,16,4,32]{0,3,2,1:T(8,128)(2,1)S(1)} %copy.120) | copy-start | bytes 786436
  90.1 3.1 %copy-start.3 = (f32[16,4,64,64]{2,3,1,0:T(8,128)S(1)}, f32[16,4,64,64]{2,3,1,0:T(8,128)}, u32[]{:S(2)}) copy-start(f32[16,4,64,64]{2,3,1,0:T(8,128)} %get-tuple-element.20) | copy-start | bytes 3145732
  90.1 3.1 %copy-start.18 = (f32[16,4,64]{2,1,0:T(4,128)S(1)}, f32[16,4,64]{2,1,0:T(4,128)}, u32[]{:S(2)}) copy-start(f32[16,4,64]{2,1,0:T(4,128)} %copy-done.17) | copy-start | bytes 49156
  113.5 2.5 copy-start.15
  113.5 3.4 %copy-start.10 = (bf16[2,32,16,128]{3,2,0,1:T(8,128)(2,1)S(1)}, bf16[2,32,16,128]{3,2,0,1:T(8,128)(2,1)}, u32[]{:S(2)}) copy-start(bf16[2,32,16,128]{3,2,0,1:T(8,128)(2,1)} %copy-done.9) | copy-start | bytes 786436
  113.5 4.3 %copy-start.2 = (bf16[1024,128]{1,0:T(8,128)(2,1)S(1)}, bf16[1024,128]{1,0:T(8,128)(2,1)}, u32[]{:S(2)}) copy-start(bf16[1024,128]{1,0:T(8,128)(2,1)} %reshape.192) | copy-start | bytes 786436
  115.1 9.0 %copy-start.8 = (bf16[1024,128]{1,0:T(8,128)(2,1)S(1)}, bf16[1024,128]{1,0:T(8,128)(2,1)}, u32[]{:S(2)}) copy-start(bf16[1024,128]{1,0:T(8,128)(2,1)} %reshape.194) | copy-start | bytes 786436
  119.6 14.9 %copy-start.12 = (bf16[512,128]{1,0:T(8,128)(2,1)S(1)}, bf16[512,128]{1,0:T(8,128)(2,1)}, u32[]{:S(2)}) copy-start(bf16[512,128]{1,0:T(8,128)(2,1)} %param.19) | copy-start | bytes 393220
  119.6 14.9 %all-to-all-start.3 = ((bf16[64,1,16,128]{3,2,1,0:T(8,128)(2,1)}), bf16[64,1,16,128]{3,2,1,0:T(8,128)(2,1)S(1)}, u32[]{:S(2)}, u32[]{:S(2)}) async-start(bf16[64,1,16,128]{3,2,1,0:T(8,128)(2,1)} %bitcast.37), calls=%async_computation.3 | async-start | bytes 524288 | tf_op jit(solution)/shard_map/all_to_all | solution.py:203
  124.1 112.3 %all-reduce.3.cloned.1.call-start = ((), (), s32[]{:S(2)}) async-start(), calls=%async_computation.5 | async-start | bytes 131072
  125.0 15.3 %copy-start.16 = (bf16[2,128,128]{2,1,0:T(8,128)(2,1)S(1)}, bf16[2,128,128]{2,1,0:T(8,128)(2,1)}, u32[]{:S(2)}) copy-start(bf16[2,128,128]{2,1,0:T(8,128)(2,1)} %param.12) | copy-start | bytes 196612
  135.6 103.2 %all-gather.3.cloned.1.call-start = ((), (), s32[]{:S(2)}) async-start(), calls=%async_computation.4 | async-start | bytes 6488064 | tf_op jit(solution)/shard_map/all_gather | solution.py:223
  141.2 15.6 %all-to-all-start.2 = ((bf16[64,1,16,128]{3,2,1,0:T(8,128)(2,1)}), bf16[64,1,16,128]{3,2,1,0:T(8,128)(2,1)S(1)}, u32[]{:S(2)}, u32[]{:S(2)}) async-start(bf16[64,1,16,128]{3,2,1,0:T(8,128)(2,1)} %bitcast.32), calls=%async_computation.2 | async-start | bytes 524288 | tf_op jit(solution)/shard_map/all_to_all | solution.py:200
  152.5 1.9 copy-start.20
  (3 other events, 3.1 us)
Sparse Core Ops, SparseCore 0:
  135.7 100.6 all-reduce.2
Sparse Core Ops, SparseCore 1:
  140.3 86.5 all-gather.2
